TPU v7x, 32 devices: a whole 2x2x4 slice. The times are simulated.
32 devices in a mesh: section: 4 (over z), dp: 4 (over x, core), space: 2 (over y).
Axes of the slice: x: 2, y: 2, z: 4, core: 2. Of those that a mesh axis runs over, the one named last changes fastest.
Arguments:
- inputs: bfloat16 [4, 2, 4, 2, 8, 8, 256], P('section', None, 'dp', 'space'), may hold values from -6 to 6
- preacts: bfloat16 [4, 2, 4, 2, 8, 8, 256], P('section', None, 'dp', 'space'), may hold values from -6 to 6
- out_grad: bfloat16 [2, 4, 2, 8, 8, 256], P(None, 'dp', 'space'), may hold values from -6 to 6
- conv_w: bfloat16 [4, 27, 256, 256], P('section'), may hold values from -0.078125 to 0.078125
- proj_w: bfloat16 [4, 256, 256], P('section'), may hold values from -0.1875 to 0.1875
Outputs:
- section_grads: bfloat16 [4, 2, 4, 2, 8, 8, 256], P('section', None, 'dp', 'space')
- grad_conv: float32 [4, 256, 27, 256], P('section', 'dp')
- grad_proj: float32 [4, 256, 256], P('section', 'dp')
All inputs are finite; a program needn't handle non-finite values.
Results may differ from a plain program's by a relative error of at most 0.029.
Values may be sent and summed in bfloat16 or wider, within the bound.
No kernel may reach another device: no remote copies, remote signals or barrier semaphores. Data moves between devices by JAX's collectives and lax.ppermute only.
A program may use at most 64 MiB of HBM per device.

v0:
```python
import functools

import jax
import jax.numpy as jnp
from jax import lax
from jax.experimental import pallas as pl
from jax.experimental.pallas import tpu as pltpu
from jax.sharding import PartitionSpec as P

SIDE = (-1, 0, 1)
PLANE_TAPS = [(row, col) for row in SIDE for col in SIDE]
VMEM_LIMIT = 16 * 1024 * 1024


def rotated(axis, distance):
    count = lax.axis_size(axis)
    return [((i + distance) % count, i) for i in range(count)]


def neighbours(block, axis):
    blocks = [block]
    for distance in range(1, lax.axis_size(axis)):
        blocks.append(lax.ppermute(block, axis, rotated(axis, distance)))
    return blocks


def shifted(plane, row_off, col_off, height, width):
    lanes = plane.shape[1]
    step = row_off * width + col_off
    moved = pltpu.roll(plane, (-step) % lanes, 1) if step % lanes else plane
    place = lax.broadcasted_iota(jnp.int32, (1, lanes), 1)
    row = (place // width) % height + row_off
    col = place % width + col_off
    inside = (row >= 0) & (row < height) & (col >= 0) & (col < width)
    return jnp.where(inside, moved, jnp.zeros((), plane.dtype))


def block_step(grad, pre, conv_ref, proj, height, width):
    planes = len(grad)
    joined = jnp.concatenate(grad, axis=1)
    hidden_grad = jnp.dot(proj, joined, preferred_element_type=jnp.float32)
    keep = jnp.concatenate(pre, axis=1).astype(jnp.float32) > 0
    masked = jnp.where(keep, hidden_grad, 0.0).astype(jnp.bfloat16).astype(jnp.float32)
    lanes = grad[0].shape[1]
    total = joined.astype(jnp.float32)
    parts = [total[:, z * lanes : (z + 1) * lanes] for z in range(planes)]
    total = jnp.concatenate(parts, axis=1)
    taps = len(PLANE_TAPS)
    for tap, (row_off, col_off) in enumerate(PLANE_TAPS):
        moved = jnp.concatenate(
            [
                shifted(
                    masked[:, z * lanes : (z + 1) * lanes], -row_off, -col_off, height, width
                ).astype(jnp.bfloat16)
                for z in range(planes)
            ],
            axis=1,
        )
        blank = jnp.zeros((moved.shape[0], lanes), jnp.bfloat16)
        for depth, depth_off in enumerate(SIDE):
            if depth_off == 0:
                source = moved
            elif depth_off > 0:
                source = jnp.concatenate([blank, moved[:, : (planes - 1) * lanes]], axis=1)
            else:
                source = jnp.concatenate([moved[:, lanes:], blank], axis=1)
            total = total + jnp.dot(
                conv_ref[depth * taps + tap], source, preferred_element_type=jnp.float32
            )
    return [total[:, z * lanes : (z + 1) * lanes].astype(jnp.bfloat16) for z in range(planes)]


def flipped(rows):
    return rows.astype(jnp.float32).T


def prepare_kernel(seed_ref, pre_ref, acts_ref, conv_ref, proj_ref, *refs):
    seed_out, pre_out, acts_out, conv_out, proj_out, seed_rows, pre_rows, acts_rows, sems = refs
    rows_copies = [
        pltpu.make_async_copy(source, target, sems.at[place])
        for place, (source, target) in enumerate(
            ((seed_ref, seed_rows), (pre_ref, pre_rows), (acts_ref, acts_rows))
        )
    ]
    weight_copies = [
        pltpu.make_async_copy(conv_ref, conv_out, sems.at[3]),
        pltpu.make_async_copy(proj_ref, proj_out, sems.at[4]),
    ]
    for copy in rows_copies + weight_copies:
        copy.start()
    channels = seed_rows.shape[-1]
    for copy, rows, out in zip(
        rows_copies, (seed_rows, pre_rows, acts_rows), (seed_out, pre_out, acts_out)
    ):
        copy.wait()
        for depth in range(out.shape[0]):
            out[depth] = flipped(rows[:, depth].reshape(-1, channels)).astype(jnp.bfloat16)
    for copy in weight_copies:
        copy.wait()


def placed_planes(here, own_ref, row_refs, target):
    depth_dev, channels = own_ref.shape[:2]
    count = len(row_refs) + 1
    for depth in range(depth_dev):
        target[here * depth_dev + depth] = own_ref[depth].astype(target.dtype)
    for distance, rows_ref in enumerate(row_refs, 1):
        place = lax.rem(here + distance, count)
        for depth in range(depth_dev):
            rows = rows_ref[:, depth].reshape(-1, channels)
            target[place * depth_dev + depth] = flipped(rows).astype(target.dtype)


def first_kernel(others, height, width, *refs):
    seed_ref, seed_rows = refs[0], refs[1 : 1 + others]
    pre_ref, pre_rows = refs[1 + others], refs[2 + others : 2 + 2 * others]
    conv_ref, proj_ref, grad_ref, pre_out_ref, out_ref = refs[2 + 2 * others :]
    here = lax.axis_index("space")
    placed_planes(here, seed_ref, seed_rows, grad_ref)
    placed_planes(here, pre_ref, pre_rows, pre_out_ref)
    step_kernel(height, width, grad_ref, pre_out_ref, conv_ref, proj_ref, out_ref)


def step_kernel(height, width, grad_ref, pre_ref, conv_ref, proj_ref, out_ref):
    planes = grad_ref.shape[0]
    result = block_step(
        [grad_ref[z] for z in range(planes)],
        [pre_ref[z] for z in range(planes)],
        conv_ref,
        proj_ref[...],
        height,
        width,
    )
    for z in range(planes):
        out_ref[z] = result[z]


def pack_kernel(others, *refs):
    pre_ref, acts_ref, acts_rows = refs[0], refs[1], refs[2 : 2 + others]
    parcel_refs, scratch = refs[2 + others : -1], refs[-1]
    here = lax.axis_index("space")
    place = lax.axis_index("dp")
    count = len(parcel_refs)
    planes, channels = pre_ref.shape[:2]
    shard = channels // count
    padded = parcel_refs[0].shape[1] - channels
    placed_planes(here, acts_ref, acts_rows, scratch)
    for distance in range(count):
        target = lax.rem(place - distance + count, count)
        for z in range(planes):
            parcel_refs[distance][z, :channels] = pre_ref[z]
            rows = scratch[z, pl.ds(pl.multiple_of(target * shard, shard), shard)]
            parcel_refs[distance][z, channels : channels + shard] = rows.astype(jnp.bfloat16)
            if padded > shard:
                parcel_refs[distance][z, channels + shard :] = jnp.zeros(
                    (padded - shard, rows.shape[1]), jnp.bfloat16
                )


def unfold_kernel(height, width, channels, shard, *refs):
    parcel_refs, unfolded_ref = refs[:-1], refs[-1]
    for place, parcel_ref in enumerate(parcel_refs):
        planes = [
            parcel_ref[z, channels:].astype(jnp.float32)[:shard]
            for z in range(parcel_ref.shape[0])
        ]
        moved = [
            [shifted(plane, row_off, col_off, height, width) for row_off, col_off in PLANE_TAPS]
            for plane in planes
        ]
        blank = jnp.zeros_like(planes[0])
        columns = []
        for z in range(len(planes)):
            taps = []
            for depth_off in SIDE:
                inside = 0 <= z + depth_off < len(planes)
                taps.extend(moved[z + depth_off] if inside else [blank] * len(PLANE_TAPS))
            columns.append(jnp.concatenate(taps, axis=0).astype(jnp.bfloat16))
        lanes = planes[0].shape[1] * len(planes)
        unfolded_ref[:, place * lanes : (place + 1) * lanes] = jnp.concatenate(columns, axis=1)


def choose_kernel(count, *refs):
    step_refs, early_ref = refs[:-1], refs[-1]
    section = lax.axis_index("section")
    for step, step_ref in enumerate(step_refs):

        @pl.when(section == count - 1 - step)
        def _(step_ref=step_ref):
            early_ref[...] = step_ref[...]

    @pl.when(section < count - len(step_refs))
    def _():
        early_ref[...] = jnp.zeros_like(early_ref)


def weights_kernel(count, scale_term, cuts, *refs):
    early_refs, late_refs = refs[:count], refs[count : 2 * count]
    parcel_refs = refs[2 * count : 3 * count]
    unfolded_ref, proj_ref, conv_out_ref, proj_out_ref, masked_ref, rows_ref, sems = refs[3 * count :]
    here = lax.axis_index("dp")
    last = lax.axis_index("section") == 0
    shard, channels = proj_out_ref.shape
    planes = parcel_refs[0].shape[0]
    contract_lanes = (((1,), (1,)), ((), ()))
    proj_total = None
    for place in range(count):
        grad = jnp.concatenate(
            [jnp.where(last, late_refs[place][z], early_refs[place][z]) for z in range(planes)],
            axis=1,
        )
        parcel_ref = parcel_refs[place]
        pre = jnp.concatenate([parcel_ref[z, :channels] for z in range(planes)], axis=1)
        hidden_grad = jnp.dot(proj_ref[...], grad, preferred_element_type=jnp.float32)
        lanes = grad.shape[1]
        masked_ref[:, place * lanes : (place + 1) * lanes] = jnp.where(
            pre.astype(jnp.float32) > 0, hidden_grad, 0.0
        ).astype(jnp.bfloat16)
        rows = pl.ds(pl.multiple_of(here * shard, shard), shard)
        mine = jnp.concatenate([parcel_ref[z, rows] for z in range(planes)], axis=1)
        hidden = jnp.maximum(mine.astype(jnp.float32), 0.0).astype(jnp.bfloat16)
        term = lax.dot_general(hidden, grad, contract_lanes, preferred_element_type=jnp.float32)
        proj_total = term if proj_total is None else proj_total + term
    proj_out_ref[...] = proj_total * scale_term
    size = rows_ref.shape[1]
    copies = []
    for cut in range(cuts):
        span = pl.ds(cut * size, size)
        total = lax.dot_general(
            unfolded_ref[span], masked_ref[...], contract_lanes, preferred_element_type=jnp.float32
        )
        rows_ref[cut] = total * scale_term
        copies.append(
            pltpu.make_async_copy(rows_ref.at[cut], conv_out_ref.at[span], sems.at[cut])
        )
        copies[-1].start()
    for copy in copies:
        copy.wait()


def select_kernel(count, depth_dev, *refs):
    out_refs, section_ref = refs[:count], refs[count]
    section = lax.axis_index("section")
    here = lax.axis_index("space")
    micro, _, area, channels = section_ref.shape
    for step in range(count):

        @pl.when(section == count - 1 - step)
        def _(step=step):
            for depth in range(depth_dev):
                plane = out_refs[step][here * depth_dev + depth].astype(jnp.float32)
                rows = plane.T.astype(jnp.bfloat16)
                for index in range(micro):
                    section_ref[index, depth] = rows[index * area : (index + 1) * area]


def whole(count=1):
    return [pl.BlockSpec(memory_space=pltpu.VMEM)] * count


def params():
    return pltpu.CompilerParams(vmem_limit_bytes=VMEM_LIMIT)


def kept_in_hbm(*arrays):
    return [pltpu.with_memory_space_constraint(array, pltpu.HBM) for array in arrays]


def shards(inputs, preacts, out_grad, conv_w, proj_w):
    section_count = lax.axis_size("section")
    crop_count = lax.axis_size("dp")
    space_count = lax.axis_size("space")
    micro, _, depth_dev, height, width, channels = inputs.shape[1:]
    area = height * width
    lanes = micro * area
    planes = space_count * depth_dev
    taps = len(SIDE) * len(PLANE_TAPS)
    shard = channels // crop_count
    others = space_count - 1
    scale_term = 1.0 / (micro * crop_count)
    local = (micro, depth_dev, area, channels)
    acts = inputs.reshape(local)
    pre_acts = preacts.reshape(local)
    seeds = out_grad.reshape(local)
    bfloat = jnp.bfloat16
    volume = jax.ShapeDtypeStruct((planes, channels, lanes), bfloat)
    slab = jax.ShapeDtypeStruct((depth_dev, channels, lanes), bfloat)
    padded = -(-shard // 16) * 16
    parcel = jax.ShapeDtypeStruct((planes, channels + padded, lanes), bfloat)

    seed_rows = neighbours(seeds, "space")[1:]
    pre_rows = neighbours(pre_acts, "space")[1:]
    acts_rows = neighbours(acts, "space")[1:]

    seed_own, pre_own, acts_own, conv_weight, proj_weight = pl.pallas_call(
        prepare_kernel,
        out_shape=(
            slab,
            slab,
            slab,
            jax.ShapeDtypeStruct(conv_w.shape[1:], bfloat),
            jax.ShapeDtypeStruct(proj_w.shape[1:], bfloat),
        ),
        in_specs=[pl.BlockSpec(memory_space=pltpu.HBM)] * 5,
        out_specs=tuple(whole(5)),
        scratch_shapes=[pltpu.VMEM(local, bfloat)] * 3 + [pltpu.SemaphoreType.DMA((5,))],
        compiler_params=params(),
        name="prepare",
    )(*kept_in_hbm(seeds, pre_acts, acts, conv_w[0], proj_w[0]))

    grad_first, pre_all, result = pl.pallas_call(
        functools.partial(first_kernel, others, height, width),
        out_shape=(volume, volume, volume),
        in_specs=whole(4 + 2 * others),
        out_specs=tuple(whole(3)),
        compiler_params=params(),
        name="first_block",
    )(seed_own, *seed_rows, pre_own, *pre_rows, conv_weight, proj_weight)

    step_call = pl.pallas_call(
        functools.partial(step_kernel, height, width),
        out_shape=volume,
        in_specs=whole(4),
        out_specs=whole()[0],
        compiler_params=params(),
        name="block",
    )
    results = [result]
    received = []
    parcels = None
    for step in range(1, section_count):
        holder = section_count - 1 - step
        received.append(lax.ppermute(results[-1], "section", [(holder + 1, holder)]))
        if parcels is None:
            sent = pl.pallas_call(
                functools.partial(pack_kernel, others),
                out_shape=(parcel,) * crop_count,
                in_specs=whole(2 + others),
                out_specs=tuple(whole(crop_count)),
                scratch_shapes=[pltpu.VMEM(volume.shape, jnp.float32)],
                compiler_params=params(),
                name="pack",
            )(pre_all, acts_own, *acts_rows)
            parcels = [sent[0]] + [
                lax.ppermute(sent[distance], "dp", rotated("dp", distance))
                for distance in range(1, crop_count)
            ]
        results.append(step_call(received[-1], pre_all, conv_weight, proj_weight))
    early = pl.pallas_call(
        functools.partial(choose_kernel, section_count),
        out_shape=volume,
        in_specs=whole(section_count - 1),
        out_specs=whole()[0],
        compiler_params=params(),
        name="choose",
    )(grad_first, *received[:-1])
    early_blocks = neighbours(early, "dp")
    late_blocks = neighbours(received[-1], "dp")

    unfolded = pl.pallas_call(
        functools.partial(unfold_kernel, height, width, channels, shard),
        out_shape=jax.ShapeDtypeStruct((taps * shard, crop_count * planes * lanes), bfloat),
        in_specs=whole(crop_count),
        out_specs=whole()[0],
        compiler_params=params(),
        name="unfold",
    )(*parcels)

    cuts = len(SIDE) if (len(PLANE_TAPS) * shard) % 16 == 0 else 1
    rows = taps * shard // cuts
    conv_rows, proj_rows = pl.pallas_call(
        functools.partial(weights_kernel, crop_count, scale_term, cuts),
        out_shape=(
            jax.ShapeDtypeStruct((taps * shard, channels), jnp.float32),
            jax.ShapeDtypeStruct((shard, channels), jnp.float32),
        ),
        in_specs=whole(3 * crop_count + 2),
        out_specs=(pl.BlockSpec(memory_space=pltpu.HBM), whole()[0]),
        scratch_shapes=[
            pltpu.VMEM((channels, crop_count * planes * lanes), bfloat),
            pltpu.VMEM((cuts, rows, channels), jnp.float32),
            pltpu.SemaphoreType.DMA((cuts,)),
        ],
        compiler_params=params(),
        name="weight_grads",
    )(*early_blocks, *late_blocks, *parcels, unfolded, proj_weight)

    section_out = pl.pallas_call(
        functools.partial(select_kernel, section_count, depth_dev),
        out_shape=jax.ShapeDtypeStruct(local, bfloat),
        in_specs=whole(section_count),
        out_specs=whole()[0],
        compiler_params=params(),
        name="own_grads",
    )(*results)

    section_grads = section_out.reshape(inputs.shape)
    grad_conv = conv_rows.reshape(taps, shard, channels).swapaxes(0, 1)[None]
    return section_grads, grad_conv, proj_rows[None]


def solution(mesh):
    placed = (
        P("section", None, "dp", "space", None, None, None),
        P("section", None, "dp", "space", None, None, None),
        P(None, "dp", "space", None, None, None),
        P("section", None, None, None),
        P("section", None, None),
    )
    return jax.shard_map(
        shards,
        mesh=mesh,
        in_specs=placed,
        out_specs=(
            P("section", None, "dp", "space", None, None, None),
            P("section", "dp", None, None),
            P("section", "dp", None),
        ),
        check_vma=False,
    )
```

profile of v0, /device:TPU:17, one launch (start us, length us, event | category | flops | bytes accessed | tf_op | source)
XLA Modules:
  0.0 46.6 jit_solution(9086761815615620807)
XLA Ops:
  0.6 1.3 %collective-permute-start.1 = (bf16[2,1,64,256]{3,2,1,0:T(8,128)(2,1)}, bf16[2,1,64,256]{3,2,1,0:T(8,128)(2,1)S(1)}, u32[]{:S(2)}, u32[]{:S(2)}) collective-permute-start(bf16[2,1,64,256]{3,2,1,0:T(8,128)(2,1)} %bitcast.16), channel_id=1, source_target_pairs={{1,0},{0,1},{3,2},{2,3},{5,4},{4,5},{7,6},{6,7},{9,8},{8,9},{11,10... | collective-permute-start | bytes 196616 | tf_op jit(solution)/shard_map/ppermute | solution.py:23
  1.9 0.2 collective-permute-start
  2.2 2.2 %prepare.1 = (bf16[1,256,128]{2,1,0:T(8,128)(2,1)S(1)}, bf16[1,256,128]{2,1,0:T(8,128)(2,1)S(1)}, bf16[1,256,128]{2,1,0:T(8,128)(2,1)S(1)}, bf16[27,256,256]{2,1,0:T(8,128)(2,1)S(1)}, bf16[256,256]{1,0:T(8,128)(2,1)S(1)}) custom-call(bf16[2,1,64,256]{3,2,1,0:T(8,128)(2,1)} %bitcast.19, bf16[2,1,64,256]{3,2,1,0:T(8,128)(2,1)} %bitcast.17, ...), custom_call_target="tpu_custom_call" | custom-call | tf_op jit(solution)/shard_map/prepare/pallas_call | solution.py:295
  4.3 0.0 collective-permute-done.1.refs_3_
  4.3 1.7 %collective-permute-done.refs_1_ = bf16[2,1,64,256]{3,2,1,0:T(8,128)(2,1)S(1)} collective-permute-done((bf16[2,1,64,256]{3,2,1,0:T(8,128)(2,1)}, bf16[2,1,64,256]{3,2,1,0:T(8,128)(2,1)S(1)}, u32[]{:S(2)}, u32[]{:S(2)}) %collective-permute-start) | collective-permute-done | bytes 65568 | tf_op jit(solution)/shard_map/ppermute | solution.py:23
  6.0 0.0 copy-start
  6.0 1.5 %first_block.1 = (bf16[2,256,128]{2,1,0:T(8,128)(2,1)S(1)}, bf16[2,256,128]{2,1,0:T(8,128)(2,1)S(1)}, bf16[2,256,128]{2,1,0:T(8,128)(2,1)S(1)}) custom-call(bf16[1,256,128]{2,1,0:T(8,128)(2,1)S(1)} %get-tuple-element.17.refs_0_, bf16[2,1,64,256]{3,2,1,0:T(8,128)(2,1)S(1)} %collective-permute-done.refs_1_, ...), custom_call_target="tpu_custom_call" | custom-call | tf_op jit(solution)/shard_map/first_block/pallas_call | solution.py:311
  7.5 1.3 %collective-permute-start.2 = (bf16[2,256,128]{2,1,0:T(8,128)(2,1)S(1)}, bf16[2,256,128]{2,1,0:T(8,128)(2,1)S(1)}, u32[]{:S(2)}, u32[]{:S(2)}) collective-permute-start(bf16[2,256,128]{2,1,0:T(8,128)(2,1)S(1)} %get-tuple-element.21.refs_0_), channel_id=1, source_target_pairs={{24,16},{25,17},{26,18},{27,19},{28,20},{29,21},{30,22},{31,23}} | collective-permute-start | bytes 393224 | tf_op jit(solution)/shard_map/ppermute | solution.py:333
  8.8 4.4 %collective-permute-done.2.grad_ref.refs_1_ = bf16[2,256,128]{2,1,0:T(8,128)(2,1)S(1)} collective-permute-done((bf16[2,256,128]{2,1,0:T(8,128)(2,1)S(1)}, bf16[2,256,128]{2,1,0:T(8,128)(2,1)S(1)}, u32[]{:S(2)}, u32[]{:S(2)}) %collective-permute-start.2) | collective-permute-done | bytes 131104 | tf_op jit(solution)/shard_map/ppermute | solution.py:333
  13.2 1.4 %block.3.refs_1_ = bf16[2,256,128]{2,1,0:T(8,128)(2,1)S(1)} custom-call(bf16[2,256,128]{2,1,0:T(8,128)(2,1)S(1)} %collective-permute-done.2.grad_ref.refs_1_, bf16[2,256,128]{2,1,0:T(8,128)(2,1)S(1)} %get-tuple-element.22.pre_ref.refs_0_, bf16[27,256,256]{2,1,0:T(8,128)(2,1)S(1)} %get-tuple-element.19.refs_4_.conv_ref, ...), custom_call_target="tpu_custom_call" | custom-call | tf_op jit(solution)/shard_map/block/pallas_call | solution.py:348
  14.6 1.3 %collective-permute-start.3 = (bf16[2,256,128]{2,1,0:T(8,128)(2,1)S(1)}, bf16[2,256,128]{2,1,0:T(8,128)(2,1)S(1)}, u32[]{:S(2)}, u32[]{:S(2)}) collective-permute-start(bf16[2,256,128]{2,1,0:T(8,128)(2,1)S(1)} %block.3.refs_1_), channel_id=1, source_target_pairs={{16,8},{17,9},{18,10},{19,11},{20,12},{21,13},{22,14},{23,15}} | collective-permute-start | bytes 393224 | tf_op jit(solution)/shard_map/ppermute | solution.py:333
  15.9 0.0 copy-done
  15.9 0.5 %collective-permute-start.11 = (bf16[2,1,64,256]{3,2,1,0:T(8,128)(2,1)S(1)}, bf16[2,1,64,256]{3,2,1,0:T(8,128)(2,1)S(1)}, u32[]{:S(2)}, u32[]{:S(2)}) collective-permute-start(bf16[2,1,64,256]{3,2,1,0:T(8,128)(2,1)S(1)} %bitcast.21), channel_id=1, source_target_pairs={{1,0},{0,1},{3,2},{2,3},{5,4},{4,5},{7,6},{6,7},{9,8},{8,9},{11,10... | collective-permute-start | bytes 196616 | tf_op jit(solution)/shard_map/ppermute | solution.py:23
  16.5 2.7 %collective-permute-done.11.refs_2_ = bf16[2,1,64,256]{3,2,1,0:T(8,128)(2,1)S(1)} collective-permute-done((bf16[2,1,64,256]{3,2,1,0:T(8,128)(2,1)S(1)}, bf16[2,1,64,256]{3,2,1,0:T(8,128)(2,1)S(1)}, u32[]{:S(2)}, u32[]{:S(2)}) %collective-permute-start.11) | collective-permute-done | bytes 65568 | tf_op jit(solution)/shard_map/ppermute | solution.py:23
  19.1 0.1 pack.1
  19.2 3.7 %collective-permute-start.12 = (bf16[2,320,128]{2,1,0:T(8,128)(2,1)S(1)}, bf16[2,320,128]{2,1,0:T(8,128)(2,1)S(1)}, u32[]{:S(2)}, u32[]{:S(2)}) collective-permute-start(bf16[2,320,128]{2,1,0:T(8,128)(2,1)S(1)} %get-tuple-element.26), channel_id=1, source_target_pairs={{2,0},{4,2},{6,4},{0,6},{3,1},{5,3},{7,5},{1,7},{10,8},{12,10},{14... | collective-permute-start | bytes 491528 | tf_op jit(solution)/shard_map/ppermute | solution.py:345
  22.9 1.2 %collective-permute-start.13 = (bf16[2,320,128]{2,1,0:T(8,128)(2,1)S(1)}, bf16[2,320,128]{2,1,0:T(8,128)(2,1)S(1)}, u32[]{:S(2)}, u32[]{:S(2)}) collective-permute-start(bf16[2,320,128]{2,1,0:T(8,128)(2,1)S(1)} %get-tuple-element.27), channel_id=1, source_target_pairs={{4,0},{6,2},{0,4},{2,6},{5,1},{7,3},{1,5},{3,7},{12,8},{14,10},{8,... | collective-permute-start | bytes 491528 | tf_op jit(solution)/shard_map/ppermute | solution.py:345
  24.1 0.5 %collective-permute-start.14 = (bf16[2,320,128]{2,1,0:T(8,128)(2,1)S(1)}, bf16[2,320,128]{2,1,0:T(8,128)(2,1)S(1)}, u32[]{:S(2)}, u32[]{:S(2)}) collective-permute-start(bf16[2,320,128]{2,1,0:T(8,128)(2,1)S(1)} %get-tuple-element.28), channel_id=1, source_target_pairs={{6,0},{0,2},{2,4},{4,6},{7,1},{1,3},{3,5},{5,7},{14,8},{8,10},{10,... | collective-permute-start | bytes 491528 | tf_op jit(solution)/shard_map/ppermute | solution.py:345
  24.6 0.0 collective-permute-done.3.grad_ref.refs_2_
  24.6 1.4 %block.4.refs_2_ = bf16[2,256,128]{2,1,0:T(8,128)(2,1)S(1)} custom-call(bf16[2,256,128]{2,1,0:T(8,128)(2,1)S(1)} %collective-permute-done.3.grad_ref.refs_2_, bf16[2,256,128]{2,1,0:T(8,128)(2,1)S(1)} %get-tuple-element.22.pre_ref.refs_0_, bf16[27,256,256]{2,1,0:T(8,128)(2,1)S(1)} %get-tuple-element.19.refs_4_.conv_ref, ...), custom_call_target="tpu_custom_call" | custom-call | tf_op jit(solution)/shard_map/block/pallas_call | solution.py:348
  26.0 0.7 %collective-permute-start.4 = (bf16[2,256,128]{2,1,0:T(8,128)(2,1)S(1)}, bf16[2,256,128]{2,1,0:T(8,128)(2,1)S(1)}, u32[]{:S(2)}, u32[]{:S(2)}) collective-permute-start(bf16[2,256,128]{2,1,0:T(8,128)(2,1)S(1)} %block.4.refs_2_), channel_id=1, source_target_pairs={{8,0},{9,1},{10,2},{11,3},{12,4},{13,5},{14,6},{15,7}} | collective-permute-start | bytes 393224 | tf_op jit(solution)/shard_map/ppermute | solution.py:333
  26.7 0.2 collective-permute-start.7
  26.9 1.8 %collective-permute-done.12.refs_1_.refs_9_ = bf16[2,320,128]{2,1,0:T(8,128)(2,1)S(1)} collective-permute-done((bf16[2,320,128]{2,1,0:T(8,128)(2,1)S(1)}, bf16[2,320,128]{2,1,0:T(8,128)(2,1)S(1)}, u32[]{:S(2)}, u32[]{:S(2)}) %collective-permute-start.12) | collective-permute-done | bytes 163872 | tf_op jit(solution)/shard_map/ppermute | solution.py:345
  28.7 0.0 collective-permute-start.6
  28.7 0.5 collective-permute-done.13.refs_2_.refs_10_
  29.1 3.7 %collective-permute-start.5 = (bf16[2,256,128]{2,1,0:T(8,128)(2,1)S(1)}, bf16[2,256,128]{2,1,0:T(8,128)(2,1)S(1)}, u32[]{:S(2)}, u32[]{:S(2)}) collective-permute-start(bf16[2,256,128]{2,1,0:T(8,128)(2,1)S(1)} %choose.1.refs_0_), channel_id=1, source_target_pairs={{2,0},{4,2},{6,4},{0,6},{3,1},{5,3},{7,5},{1,7},{10,8},{12,10},{14... | collective-permute-start | bytes 393224 | tf_op jit(solution)/shard_map/ppermute | solution.py:23
  32.9 0.0 collective-permute-done.4.grad_ref.refs_4_
  32.9 0.0 collective-permute-start.10
  32.9 0.0 collective-permute-done.14.refs_3_.refs_11_
  32.9 1.4 %collective-permute-start.9 = (bf16[2,256,128]{2,1,0:T(8,128)(2,1)S(1)}, bf16[2,256,128]{2,1,0:T(8,128)(2,1)S(1)}, u32[]{:S(2)}, u32[]{:S(2)}) collective-permute-start(bf16[2,256,128]{2,1,0:T(8,128)(2,1)S(1)} %collective-permute-done.4.grad_ref.refs_4_), channel_id=1, source_target_pairs={{4,0},{6,2},{0,4},{2,6},{5,1},{7,3},{1,5},{3,7},{12,8},{14,10},{8,... | collective-permute-start | bytes 393224 | tf_op jit(solution)/shard_map/ppermute | solution.py:23
  34.3 0.0 collective-permute-done.7.refs_3_
  34.3 1.6 %collective-permute-start.8 = (bf16[2,256,128]{2,1,0:T(8,128)(2,1)S(1)}, bf16[2,256,128]{2,1,0:T(8,128)(2,1)S(1)}, u32[]{:S(2)}, u32[]{:S(2)}) collective-permute-start(bf16[2,256,128]{2,1,0:T(8,128)(2,1)S(1)} %collective-permute-done.4.grad_ref.refs_4_), channel_id=1, source_target_pairs={{2,0},{4,2},{6,4},{0,6},{3,1},{5,3},{7,5},{1,7},{10,8},{12,10},{14... | collective-permute-start | bytes 393224 | tf_op jit(solution)/shard_map/ppermute | solution.py:23
  35.9 0.5 %unfold.1.refs_12_ = bf16[1728,1024]{1,0:T(8,128)(2,1)S(1)} custom-call(bf16[2,320,128]{2,1,0:T(8,128)(2,1)S(1)} %get-tuple-element.25.refs_0_.refs_8_, bf16[2,320,128]{2,1,0:T(8,128)(2,1)S(1)} %collective-permute-done.12.refs_1_.refs_9_, bf16[2,320,128]{2,1,0:T(8,128)(2,1)S(1)} %collective-permute-done.13.refs_2_.refs_10_, ...), custom_call_target="tpu_custom_call" | custom-call | tf_op jit(solution)/shard_map/unfold/pallas_call | solution.py:360
  36.4 1.4 %block.5.refs_3_ = bf16[2,256,128]{2,1,0:T(8,128)(2,1)S(1)} custom-call(bf16[2,256,128]{2,1,0:T(8,128)(2,1)S(1)} %collective-permute-done.4.grad_ref.refs_4_, bf16[2,256,128]{2,1,0:T(8,128)(2,1)S(1)} %get-tuple-element.22.pre_ref.refs_0_, bf16[27,256,256]{2,1,0:T(8,128)(2,1)S(1)} %get-tuple-element.19.refs_4_.conv_ref, ...), custom_call_target="tpu_custom_call" | custom-call | tf_op jit(solution)/shard_map/block/pallas_call | solution.py:348
  37.8 0.8 %own_grads.1 = bf16[2,1,64,256]{3,2,1,0:T(8,128)(2,1)} custom-call(bf16[2,256,128]{2,1,0:T(8,128)(2,1)S(1)} %get-tuple-element.21.refs_0_, bf16[2,256,128]{2,1,0:T(8,128)(2,1)S(1)} %block.3.refs_1_, bf16[2,256,128]{2,1,0:T(8,128)(2,1)S(1)} %block.4.refs_2_, bf16[2,256,128]{2,1,0:T(8,128)(2,1)S(1)} %block.5.refs_3_), custom_call_target="tpu_custom_call" | custom-call | tf_op jit(solution)/shard_map/own_grads/pallas_call | solution.py:388
  38.5 0.0 collective-permute-done.6.refs_2_
  38.5 0.0 collective-permute-done.5.refs_1_
  38.5 0.3 collective-permute-done.10.refs_7_
  38.8 4.7 %collective-permute-done.9.refs_6_ = bf16[2,256,128]{2,1,0:T(8,128)(2,1)S(1)} collective-permute-done((bf16[2,256,128]{2,1,0:T(8,128)(2,1)S(1)}, bf16[2,256,128]{2,1,0:T(8,128)(2,1)S(1)}, u32[]{:S(2)}, u32[]{:S(2)}) %collective-permute-start.9) | collective-permute-done | bytes 131104 | tf_op jit(solution)/shard_map/ppermute | solution.py:23
  43.5 0.0 collective-permute-done.8.refs_5_
  43.5 3.1 %weight_grads.1 = (f32[1728,256]{1,0:T(8,128)}, f32[64,256]{1,0:T(8,128)}) custom-call(bf16[2,256,128]{2,1,0:T(8,128)(2,1)S(1)} %choose.1.refs_0_, bf16[2,256,128]{2,1,0:T(8,128)(2,1)S(1)} %collective-permute-done.5.refs_1_, bf16[2,256,128]{2,1,0:T(8,128)(2,1)S(1)} %collective-permute-done.6.refs_2_, ...), custom_call_target="tpu_custom_call" | custom-call | tf_op jit(solution)/shard_map/weight_grads/pallas_call | solution.py:371
  (1 shorter events, 0.0 us)
Async XLA Ops:
  0.6 3.7 %collective-permute-start.1 = (bf16[2,1,64,256]{3,2,1,0:T(8,128)(2,1)}, bf16[2,1,64,256]{3,2,1,0:T(8,128)(2,1)S(1)}, u32[]{:S(2)}, u32[]{:S(2)}) collective-permute-start(bf16[2,1,64,256]{3,2,1,0:T(8,128)(2,1)} %bitcast.16), channel_id=1, source_target_pairs={{1,0},{0,1},{3,2},{2,3},{5,4},{4,5},{7,6},{6,7},{9,8},{8,9},{11,10... | collective-permute-start | bytes 196616 | tf_op jit(solution)/shard_map/ppermute | solution.py:23
  1.9 4.1 %collective-permute-start = (bf16[2,1,64,256]{3,2,1,0:T(8,128)(2,1)}, bf16[2,1,64,256]{3,2,1,0:T(8,128)(2,1)S(1)}, u32[]{:S(2)}, u32[]{:S(2)}) collective-permute-start(bf16[2,1,64,256]{3,2,1,0:T(8,128)(2,1)} %bitcast.18), channel_id=1, source_target_pairs={{1,0},{0,1},{3,2},{2,3},{5,4},{4,5},{7,6},{6,7},{9,8},{8,9},{11,10... | collective-permute-start | bytes 196616 | tf_op jit(solution)/shard_map/ppermute | solution.py:23
  6.0 9.9 %copy-start = (bf16[1,2,1,1,8,8,256]{6,5,4,3,2,1,0:T(8,128)(2,1)S(1)}, bf16[1,2,1,1,8,8,256]{6,5,4,3,2,1,0:T(8,128)(2,1)}, u32[]{:S(2)}) copy-start(bf16[1,2,1,1,8,8,256]{6,5,4,3,2,1,0:T(8,128)(2,1)} %param.5) | copy-start | bytes 196612
  7.5 5.7 %collective-permute-start.2 = (bf16[2,256,128]{2,1,0:T(8,128)(2,1)S(1)}, bf16[2,256,128]{2,1,0:T(8,128)(2,1)S(1)}, u32[]{:S(2)}, u32[]{:S(2)}) collective-permute-start(bf16[2,256,128]{2,1,0:T(8,128)(2,1)S(1)} %get-tuple-element.21.refs_0_), channel_id=1, source_target_pairs={{24,16},{25,17},{26,18},{27,19},{28,20},{29,21},{30,22},{31,23}} | collective-permute-start | bytes 393224 | tf_op jit(solution)/shard_map/ppermute | solution.py:333
  14.6 10.0 %collective-permute-start.3 = (bf16[2,256,128]{2,1,0:T(8,128)(2,1)S(1)}, bf16[2,256,128]{2,1,0:T(8,128)(2,1)S(1)}, u32[]{:S(2)}, u32[]{:S(2)}) collective-permute-start(bf16[2,256,128]{2,1,0:T(8,128)(2,1)S(1)} %block.3.refs_1_), channel_id=1, source_target_pairs={{16,8},{17,9},{18,10},{19,11},{20,12},{21,13},{22,14},{23,15}} | collective-permute-start | bytes 393224 | tf_op jit(solution)/shard_map/ppermute | solution.py:333
  15.9 3.2 %collective-permute-start.11 = (bf16[2,1,64,256]{3,2,1,0:T(8,128)(2,1)S(1)}, bf16[2,1,64,256]{3,2,1,0:T(8,128)(2,1)S(1)}, u32[]{:S(2)}, u32[]{:S(2)}) collective-permute-start(bf16[2,1,64,256]{3,2,1,0:T(8,128)(2,1)S(1)} %bitcast.21), channel_id=1, source_target_pairs={{1,0},{0,1},{3,2},{2,3},{5,4},{4,5},{7,6},{6,7},{9,8},{8,9},{11,10... | collective-permute-start | bytes 196616 | tf_op jit(solution)/shard_map/ppermute | solution.py:23
  19.2 9.4 %collective-permute-start.12 = (bf16[2,320,128]{2,1,0:T(8,128)(2,1)S(1)}, bf16[2,320,128]{2,1,0:T(8,128)(2,1)S(1)}, u32[]{:S(2)}, u32[]{:S(2)}) collective-permute-start(bf16[2,320,128]{2,1,0:T(8,128)(2,1)S(1)} %get-tuple-element.26), channel_id=1, source_target_pairs={{2,0},{4,2},{6,4},{0,6},{3,1},{5,3},{7,5},{1,7},{10,8},{12,10},{14... | collective-permute-start | bytes 491528 | tf_op jit(solution)/shard_map/ppermute | solution.py:345
  22.9 6.2 %collective-permute-start.13 = (bf16[2,320,128]{2,1,0:T(8,128)(2,1)S(1)}, bf16[2,320,128]{2,1,0:T(8,128)(2,1)S(1)}, u32[]{:S(2)}, u32[]{:S(2)}) collective-permute-start(bf16[2,320,128]{2,1,0:T(8,128)(2,1)S(1)} %get-tuple-element.27), channel_id=1, source_target_pairs={{4,0},{6,2},{0,4},{2,6},{5,1},{7,3},{1,5},{3,7},{12,8},{14,10},{8,... | collective-permute-start | bytes 491528 | tf_op jit(solution)/shard_map/ppermute | solution.py:345
  24.1 8.8 %collective-permute-start.14 = (bf16[2,320,128]{2,1,0:T(8,128)(2,1)S(1)}, bf16[2,320,128]{2,1,0:T(8,128)(2,1)S(1)}, u32[]{:S(2)}, u32[]{:S(2)}) collective-permute-start(bf16[2,320,128]{2,1,0:T(8,128)(2,1)S(1)} %get-tuple-element.28), channel_id=1, source_target_pairs={{6,0},{0,2},{2,4},{4,6},{7,1},{1,3},{3,5},{5,7},{14,8},{8,10},{10,... | collective-permute-start | bytes 491528 | tf_op jit(solution)/shard_map/ppermute | solution.py:345
  26.0 6.9 %collective-permute-start.4 = (bf16[2,256,128]{2,1,0:T(8,128)(2,1)S(1)}, bf16[2,256,128]{2,1,0:T(8,128)(2,1)S(1)}, u32[]{:S(2)}, u32[]{:S(2)}) collective-permute-start(bf16[2,256,128]{2,1,0:T(8,128)(2,1)S(1)} %block.4.refs_2_), channel_id=1, source_target_pairs={{8,0},{9,1},{10,2},{11,3},{12,4},{13,5},{14,6},{15,7}} | collective-permute-start | bytes 393224 | tf_op jit(solution)/shard_map/ppermute | solution.py:333
  26.7 7.5 %collective-permute-start.7 = (bf16[2,256,128]{2,1,0:T(8,128)(2,1)S(1)}, bf16[2,256,128]{2,1,0:T(8,128)(2,1)S(1)}, u32[]{:S(2)}, u32[]{:S(2)}) collective-permute-start(bf16[2,256,128]{2,1,0:T(8,128)(2,1)S(1)} %choose.1.refs_0_), channel_id=1, source_target_pairs={{6,0},{0,2},{2,4},{4,6},{7,1},{1,3},{3,5},{5,7},{14,8},{8,10},{10,... | collective-permute-start | bytes 393224 | tf_op jit(solution)/shard_map/ppermute | solution.py:23
  28.7 9.8 %collective-permute-start.6 = (bf16[2,256,128]{2,1,0:T(8,128)(2,1)S(1)}, bf16[2,256,128]{2,1,0:T(8,128)(2,1)S(1)}, u32[]{:S(2)}, u32[]{:S(2)}) collective-permute-start(bf16[2,256,128]{2,1,0:T(8,128)(2,1)S(1)} %choose.1.refs_0_), channel_id=1, source_target_pairs={{4,0},{6,2},{0,4},{2,6},{5,1},{7,3},{1,5},{3,7},{12,8},{14,10},{8,... | collective-permute-start | bytes 393224 | tf_op jit(solution)/shard_map/ppermute | solution.py:23
  29.1 9.4 %collective-permute-start.5 = (bf16[2,256,128]{2,1,0:T(8,128)(2,1)S(1)}, bf16[2,256,128]{2,1,0:T(8,128)(2,1)S(1)}, u32[]{:S(2)}, u32[]{:S(2)}) collective-permute-start(bf16[2,256,128]{2,1,0:T(8,128)(2,1)S(1)} %choose.1.refs_0_), channel_id=1, source_target_pairs={{2,0},{4,2},{6,4},{0,6},{3,1},{5,3},{7,5},{1,7},{10,8},{12,10},{14... | collective-permute-start | bytes 393224 | tf_op jit(solution)/shard_map/ppermute | solution.py:23
  32.9 5.9 %collective-permute-start.10 = (bf16[2,256,128]{2,1,0:T(8,128)(2,1)S(1)}, bf16[2,256,128]{2,1,0:T(8,128)(2,1)S(1)}, u32[]{:S(2)}, u32[]{:S(2)}) collective-permute-start(bf16[2,256,128]{2,1,0:T(8,128)(2,1)S(1)} %collective-permute-done.4.grad_ref.refs_4_), channel_id=1, source_target_pairs={{6,0},{0,2},{2,4},{4,6},{7,1},{1,3},{3,5},{5,7},{14,8},{8,10},{10,... | collective-permute-start | bytes 393224 | tf_op jit(solution)/shard_map/ppermute | solution.py:23
  32.9 10.6 %collective-permute-start.9 = (bf16[2,256,128]{2,1,0:T(8,128)(2,1)S(1)}, bf16[2,256,128]{2,1,0:T(8,128)(2,1)S(1)}, u32[]{:S(2)}, u32[]{:S(2)}) collective-permute-start(bf16[2,256,128]{2,1,0:T(8,128)(2,1)S(1)} %collective-permute-done.4.grad_ref.refs_4_), channel_id=1, source_target_pairs={{4,0},{6,2},{0,4},{2,6},{5,1},{7,3},{1,5},{3,7},{12,8},{14,10},{8,... | collective-permute-start | bytes 393224 | tf_op jit(solution)/shard_map/ppermute | solution.py:23
  34.3 9.3 %collective-permute-start.8 = (bf16[2,256,128]{2,1,0:T(8,128)(2,1)S(1)}, bf16[2,256,128]{2,1,0:T(8,128)(2,1)S(1)}, u32[]{:S(2)}, u32[]{:S(2)}) collective-permute-start(bf16[2,256,128]{2,1,0:T(8,128)(2,1)S(1)} %collective-permute-done.4.grad_ref.refs_4_), channel_id=1, source_target_pairs={{2,0},{4,2},{6,4},{0,6},{3,1},{5,3},{7,5},{1,7},{10,8},{12,10},{14... | collective-permute-start | bytes 393224 | tf_op jit(solution)/shard_map/ppermute | solution.py:23
where the time goes:
time: 46.8 us; the launch traced here: 46.6 us
  starting transfers between devices  17.6 us (38%)
  waiting for transfers between devices  16 us (34%)
  Pallas kernels  12.3 us (26%)
  between operations  0.72 us (2%)
    ppermute x9, waiting for transfers between devices, neighbours(): blocks.append(lax.ppermute(block, axis, rotated(axis, distance)))  9.35 us
    ppermute x9, starting transfers between devices, neighbours(): blocks.append(lax.ppermute(block, axis, rotated(axis, distance)))  8.98 us
    ppermute x3, starting transfers between devices, shards(): lax.ppermute(sent[distance], 'dp', rotated('dp', distance))  5.38 us
    ppermute x3, waiting for transfers between devices, shards(): lax.ppermute(results[-1], 'section', [(holder + 1, holder)])  4.42 us
    pallas_call x3, Pallas kernels, shards(): results.append(step_call(received[-1], pre_all, conv_weight, proj_weight))  4.11 us
    ppermute x3, starting transfers between devices, shards(): lax.ppermute(results[-1], 'section', [(holder + 1, holder)])  3.26 us
    pallas_call x1, Pallas kernels, shards(): pl.pallas_call(functools.partial(weights_kernel, crop_count, scale_term,...  3.06 us
    ppermute x3, waiting for transfers between devices, shards(): lax.ppermute(sent[distance], 'dp', rotated('dp', distance))  2.21 us
  transfers between devices with their start and end apart: 15, of which 7 were waited for; matrix products, arithmetic and copies ran while one was open for 0% of the time, Pallas kernels for 14%

commit v1 on v0

--- a/solution.py
+++ b/solution.py
@@ -9,18 +9,22 @@
 
 SIDE = (-1, 0, 1)
 PLANE_TAPS = [(row, col) for row in SIDE for col in SIDE]
+CONTRACT_LANES = (((1,), (1,)), ((), ()))
 VMEM_LIMIT = 16 * 1024 * 1024
 
 
-def rotated(axis, distance):
+def peer(here, distance, count, back=False):
+    if count & (count - 1) == 0:
+        return here ^ distance
+    return (here + (count - distance if back else distance)) % count
+
+
+def neighbours(block, axis):
     count = lax.axis_size(axis)
-    return [((i + distance) % count, i) for i in range(count)]
-
-
-def neighbours(block, axis):
     blocks = [block]
-    for distance in range(1, lax.axis_size(axis)):
-        blocks.append(lax.ppermute(block, axis, rotated(axis, distance)))
+    for distance in range(1, count):
+        pairs = [(peer(i, distance, count), i) for i in range(count)]
+        blocks.append(lax.ppermute(block, axis, pairs))
     return blocks
 
 
@@ -105,7 +109,7 @@
     for depth in range(depth_dev):
         target[here * depth_dev + depth] = own_ref[depth].astype(target.dtype)
     for distance, rows_ref in enumerate(row_refs, 1):
-        place = lax.rem(here + distance, count)
+        place = peer(here, distance, count)
         for depth in range(depth_dev):
             rows = rows_ref[:, depth].reshape(-1, channels)
             target[place * depth_dev + depth] = flipped(rows).astype(target.dtype)
@@ -146,7 +150,7 @@
     padded = parcel_refs[0].shape[1] - channels
     placed_planes(here, acts_ref, acts_rows, scratch)
     for distance in range(count):
-        target = lax.rem(place - distance + count, count)
+        target = peer(place, distance, count, back=True)
         for z in range(planes):
             parcel_refs[distance][z, :channels] = pre_ref[z]
             rows = scratch[z, pl.ds(pl.multiple_of(target * shard, shard), shard)]
@@ -157,8 +161,8 @@
                 )
 
 
-def unfold_kernel(height, width, channels, shard, *refs):
-    parcel_refs, unfolded_ref = refs[:-1], refs[-1]
+def unfold_kernel(height, width, channels, shard, near, *refs):
+    parcel_refs, near_ref, far_ref = refs[:-2], refs[-2], refs[-1]
     for place, parcel_ref in enumerate(parcel_refs):
         planes = [
             parcel_ref[z, channels:].astype(jnp.float32)[:shard]
@@ -177,39 +181,26 @@
                 taps.extend(moved[z + depth_off] if inside else [blank] * len(PLANE_TAPS))
             columns.append(jnp.concatenate(taps, axis=0).astype(jnp.bfloat16))
         lanes = planes[0].shape[1] * len(planes)
-        unfolded_ref[:, place * lanes : (place + 1) * lanes] = jnp.concatenate(columns, axis=1)
+        target, start = (near_ref, place) if place < near else (far_ref, place - near)
+        target[:, start * lanes : (start + 1) * lanes] = jnp.concatenate(columns, axis=1)
 
 
 def choose_kernel(count, *refs):
-    step_refs, early_ref = refs[:-1], refs[-1]
+    step_refs, grad_ref = refs[:-1], refs[-1]
     section = lax.axis_index("section")
     for step, step_ref in enumerate(step_refs):
 
         @pl.when(section == count - 1 - step)
         def _(step_ref=step_ref):
-            early_ref[...] = step_ref[...]
-
-    @pl.when(section < count - len(step_refs))
-    def _():
-        early_ref[...] = jnp.zeros_like(early_ref)
-
-
-def weights_kernel(count, scale_term, cuts, *refs):
-    early_refs, late_refs = refs[:count], refs[count : 2 * count]
-    parcel_refs = refs[2 * count : 3 * count]
-    unfolded_ref, proj_ref, conv_out_ref, proj_out_ref, masked_ref, rows_ref, sems = refs[3 * count :]
+            grad_ref[...] = step_ref[...]
+
+
+def block_terms(grad_refs, parcel_refs, proj_ref, masked_ref, channels, shard):
     here = lax.axis_index("dp")
-    last = lax.axis_index("section") == 0
-    shard, channels = proj_out_ref.shape
-    planes = parcel_refs[0].shape[0]
-    contract_lanes = (((1,), (1,)), ((), ()))
-    proj_total = None
-    for place in range(count):
-        grad = jnp.concatenate(
-            [jnp.where(last, late_refs[place][z], early_refs[place][z]) for z in range(planes)],
-            axis=1,
-        )
-        parcel_ref = parcel_refs[place]
+    total = None
+    for place, (grad_ref, parcel_ref) in enumerate(zip(grad_refs, parcel_refs)):
+        planes = grad_ref.shape[0]
+        grad = jnp.concatenate([grad_ref[z] for z in range(planes)], axis=1)
         pre = jnp.concatenate([parcel_ref[z, :channels] for z in range(planes)], axis=1)
         hidden_grad = jnp.dot(proj_ref[...], grad, preferred_element_type=jnp.float32)
         lanes = grad.shape[1]
@@ -219,15 +210,36 @@
         rows = pl.ds(pl.multiple_of(here * shard, shard), shard)
         mine = jnp.concatenate([parcel_ref[z, rows] for z in range(planes)], axis=1)
         hidden = jnp.maximum(mine.astype(jnp.float32), 0.0).astype(jnp.bfloat16)
-        term = lax.dot_general(hidden, grad, contract_lanes, preferred_element_type=jnp.float32)
-        proj_total = term if proj_total is None else proj_total + term
-    proj_out_ref[...] = proj_total * scale_term
+        term = lax.dot_general(
+            hidden, grad, CONTRACT_LANES, preferred_element_type=jnp.float32
+        )
+        total = term if total is None else total + term
+    return total
+
+
+def near_kernel(count, channels, shard, *refs):
+    grad_refs, parcel_refs = refs[:count], refs[count : 2 * count]
+    unfolded_ref, proj_ref, conv_out_ref, proj_out_ref, masked_ref = refs[2 * count :]
+    proj_out_ref[...] = block_terms(
+        grad_refs, parcel_refs, proj_ref, masked_ref, channels, shard
+    )
+    conv_out_ref[...] = lax.dot_general(
+        unfolded_ref[...], masked_ref[...], CONTRACT_LANES, preferred_element_type=jnp.float32
+    )
+
+
+def far_kernel(count, channels, shard, scale_term, cuts, *refs):
+    grad_refs, parcel_refs = refs[:count], refs[count : 2 * count]
+    unfolded_ref, proj_ref, conv_near_ref, proj_near_ref = refs[2 * count : 2 * count + 4]
+    conv_out_ref, proj_out_ref, masked_ref, rows_ref, sems = refs[2 * count + 4 :]
+    proj_far = block_terms(grad_refs, parcel_refs, proj_ref, masked_ref, channels, shard)
+    proj_out_ref[...] = (proj_near_ref[...] + proj_far) * scale_term
     size = rows_ref.shape[1]
     copies = []
     for cut in range(cuts):
         span = pl.ds(cut * size, size)
-        total = lax.dot_general(
-            unfolded_ref[span], masked_ref[...], contract_lanes, preferred_element_type=jnp.float32
+        total = conv_near_ref[span] + lax.dot_general(
+            unfolded_ref[span], masked_ref[...], CONTRACT_LANES, preferred_element_type=jnp.float32
         )
         rows_ref[cut] = total * scale_term
         copies.append(
@@ -342,48 +354,65 @@
                 name="pack",
             )(pre_all, acts_own, *acts_rows)
             parcels = [sent[0]] + [
-                lax.ppermute(sent[distance], "dp", rotated("dp", distance))
+                lax.ppermute(
+                    sent[distance],
+                    "dp",
+                    [(peer(i, distance, crop_count), i) for i in range(crop_count)],
+                )
                 for distance in range(1, crop_count)
             ]
         results.append(step_call(received[-1], pre_all, conv_weight, proj_weight))
-    early = pl.pallas_call(
+    grad_own = pl.pallas_call(
         functools.partial(choose_kernel, section_count),
         out_shape=volume,
-        in_specs=whole(section_count - 1),
+        in_specs=whole(section_count),
         out_specs=whole()[0],
         compiler_params=params(),
         name="choose",
-    )(grad_first, *received[:-1])
-    early_blocks = neighbours(early, "dp")
-    late_blocks = neighbours(received[-1], "dp")
-
-    unfolded = pl.pallas_call(
-        functools.partial(unfold_kernel, height, width, channels, shard),
-        out_shape=jax.ShapeDtypeStruct((taps * shard, crop_count * planes * lanes), bfloat),
+    )(grad_first, *received)
+    grad_blocks = neighbours(grad_own, "dp")
+
+    near = crop_count // 2
+    span = planes * lanes
+    near_unfolded, far_unfolded = pl.pallas_call(
+        functools.partial(unfold_kernel, height, width, channels, shard, near),
+        out_shape=(
+            jax.ShapeDtypeStruct((taps * shard, near * span), bfloat),
+            jax.ShapeDtypeStruct((taps * shard, (crop_count - near) * span), bfloat),
+        ),
         in_specs=whole(crop_count),
-        out_specs=whole()[0],
+        out_specs=tuple(whole(2)),
         compiler_params=params(),
         name="unfold",
     )(*parcels)
 
+    conv_shape = jax.ShapeDtypeStruct((taps * shard, channels), jnp.float32)
+    proj_shape = jax.ShapeDtypeStruct((shard, channels), jnp.float32)
+    conv_near, proj_near = pl.pallas_call(
+        functools.partial(near_kernel, near, channels, shard),
+        out_shape=(conv_shape, proj_shape),
+        in_specs=whole(2 * near + 2),
+        out_specs=tuple(whole(2)),
+        scratch_shapes=[pltpu.VMEM((channels, near * span), bfloat)],
+        compiler_params=params(),
+        name="near_weight_grads",
+    )(*grad_blocks[:near], *parcels[:near], near_unfolded, proj_weight)
+
     cuts = len(SIDE) if (len(PLANE_TAPS) * shard) % 16 == 0 else 1
-    rows = taps * shard // cuts
+    far = crop_count - near
     conv_rows, proj_rows = pl.pallas_call(
-        functools.partial(weights_kernel, crop_count, scale_term, cuts),
-        out_shape=(
-            jax.ShapeDtypeStruct((taps * shard, channels), jnp.float32),
-            jax.ShapeDtypeStruct((shard, channels), jnp.float32),
-        ),
-        in_specs=whole(3 * crop_count + 2),
+        functools.partial(far_kernel, far, channels, shard, scale_term, cuts),
+        out_shape=(conv_shape, proj_shape),
+        in_specs=whole(2 * far + 4),
         out_specs=(pl.BlockSpec(memory_space=pltpu.HBM), whole()[0]),
         scratch_shapes=[
-            pltpu.VMEM((channels, crop_count * planes * lanes), bfloat),
-            pltpu.VMEM((cuts, rows, channels), jnp.float32),
+            pltpu.VMEM((channels, far * span), bfloat),
+            pltpu.VMEM((cuts, taps * shard // cuts, channels), jnp.float32),
             pltpu.SemaphoreType.DMA((cuts,)),
         ],
         compiler_params=params(),
-        name="weight_grads",
-    )(*early_blocks, *late_blocks, *parcels, unfolded, proj_weight)
+        name="far_weight_grads",
+    )(*grad_blocks[near:], *parcels[near:], far_unfolded, proj_weight, conv_near, proj_near)
 
     section_out = pl.pallas_call(
         functools.partial(select_kernel, section_count, depth_dev),

time: 46.8 us -> 42.2 us (0.902)
  the two profiles are of different devices: /device:TPU:17 before, /device:TPU:0 now
where the time goes in v1:
time: 42.2 us; the launch traced here: 42 us
  waiting for transfers between devices  17.7 us (42%)
  Pallas kernels  12.3 us (29%)
  starting transfers between devices  11.3 us (27%)
  between operations  0.74 us (2%)
    ppermute x3, waiting for transfers between devices, shards(): lax.ppermute(results[-1], 'section', [(holder + 1, holder)])  9.05 us
    ppermute x6, waiting for transfers between devices, neighbours(): blocks.append(lax.ppermute(block, axis, pairs))  8.64 us
    ppermute x6, starting transfers between devices, neighbours(): blocks.append(lax.ppermute(block, axis, pairs))  6.36 us
    pallas_call x3, Pallas kernels, shards(): results.append(step_call(received[-1], pre_all, conv_weight, proj_weight))  4.11 us
    ppermute x3, starting transfers between devices, shards(): lax.ppermute(results[-1], 'section', [(holder + 1, holder)])  2.63 us
    pallas_call x1, Pallas kernels, shards(): pl.pallas_call(functools.partial(far_kernel, far, channels, shard, scale_...  2.45 us
    ppermute x3, starting transfers between devices, shards(): lax.ppermute(sent[distance], 'dp', [(peer(i, distance, crop_count), i) fo...  2.27 us
    pallas_call x1, Pallas kernels, shards(): pl.pallas_call(prepare_kernel, out_shape=(slab, slab, slab, jax.ShapeDtyp...  2.16 us
  transfers between devices with their start and end apart: 12, of which 5 were waited for; matrix products, arithmetic and copies ran while one was open for 0% of the time, Pallas kernels for 17%

profile of v1, /device:TPU:0, one launch (start us, length us, event | category | flops | bytes accessed | tf_op | source)
XLA Modules:
  0.0 42.0 jit_solution(12483395326063962246)
XLA Ops:
  0.6 3.0 %collective-permute-start.1 = (bf16[2,1,64,256]{3,2,1,0:T(8,128)(2,1)}, bf16[2,1,64,256]{3,2,1,0:T(8,128)(2,1)S(1)}, u32[]{:S(2)}, u32[]{:S(2)}) collective-permute-start(bf16[2,1,64,256]{3,2,1,0:T(8,128)(2,1)} %bitcast.16), channel_id=1, source_target_pairs={{1,0},{0,1},{3,2},{2,3},{5,4},{4,5},{7,6},{6,7},{9,8},{8,9},{11,10... | collective-permute-start | bytes 196616 | tf_op jit(solution)/shard_map/ppermute | solution.py:27
  3.7 0.1 collective-permute-start
  3.7 2.2 %prepare.1 = (bf16[1,256,128]{2,1,0:T(8,128)(2,1)S(1)}, bf16[1,256,128]{2,1,0:T(8,128)(2,1)S(1)}, bf16[1,256,128]{2,1,0:T(8,128)(2,1)S(1)}, bf16[27,256,256]{2,1,0:T(8,128)(2,1)S(1)}, bf16[256,256]{1,0:T(8,128)(2,1)S(1)}) custom-call(bf16[2,1,64,256]{3,2,1,0:T(8,128)(2,1)} %bitcast.19, bf16[2,1,64,256]{3,2,1,0:T(8,128)(2,1)} %bitcast.17, ...), custom_call_target="tpu_custom_call" | custom-call | tf_op jit(solution)/shard_map/prepare/pallas_call | solution.py:307
  5.9 0.4 collective-permute-done.1.refs_3_
  6.3 1.9 %collective-permute-done.refs_1_ = bf16[2,1,64,256]{3,2,1,0:T(8,128)(2,1)S(1)} collective-permute-done((bf16[2,1,64,256]{3,2,1,0:T(8,128)(2,1)}, bf16[2,1,64,256]{3,2,1,0:T(8,128)(2,1)S(1)}, u32[]{:S(2)}, u32[]{:S(2)}) %collective-permute-start) | collective-permute-done | bytes 65568 | tf_op jit(solution)/shard_map/ppermute | solution.py:27
  8.1 1.5 %first_block.1 = (bf16[2,256,128]{2,1,0:T(8,128)(2,1)S(1)}, bf16[2,256,128]{2,1,0:T(8,128)(2,1)S(1)}, bf16[2,256,128]{2,1,0:T(8,128)(2,1)S(1)}) custom-call(bf16[1,256,128]{2,1,0:T(8,128)(2,1)S(1)} %get-tuple-element.21.refs_0_, bf16[2,1,64,256]{3,2,1,0:T(8,128)(2,1)S(1)} %collective-permute-done.refs_1_, ...), custom_call_target="tpu_custom_call" | custom-call | tf_op jit(solution)/shard_map/first_block/pallas_call | solution.py:323
  9.6 0.7 %collective-permute-start.2 = (bf16[2,256,128]{2,1,0:T(8,128)(2,1)S(1)}, bf16[2,256,128]{2,1,0:T(8,128)(2,1)S(1)}, u32[]{:S(2)}, u32[]{:S(2)}) collective-permute-start(bf16[2,256,128]{2,1,0:T(8,128)(2,1)S(1)} %get-tuple-element.25.refs_0_), channel_id=1, source_target_pairs={{24,16},{25,17},{26,18},{27,19},{28,20},{29,21},{30,22},{31,23}} | collective-permute-start | bytes 393224 | tf_op jit(solution)/shard_map/ppermute | solution.py:345
  10.3 0.0 collective-permute-done.2.grad_ref.refs_1_
  10.3 0.0 copy-start
  10.3 1.4 %block.3.refs_1_ = bf16[2,256,128]{2,1,0:T(8,128)(2,1)S(1)} custom-call(bf16[2,256,128]{2,1,0:T(8,128)(2,1)S(1)} %collective-permute-done.2.grad_ref.refs_1_, bf16[2,256,128]{2,1,0:T(8,128)(2,1)S(1)} %get-tuple-element.26.pre_ref.refs_0_, bf16[27,256,256]{2,1,0:T(8,128)(2,1)S(1)} %get-tuple-element.23.refs_4_.conv_ref, ...), custom_call_target="tpu_custom_call" | custom-call | tf_op jit(solution)/shard_map/block/pallas_call | solution.py:364
  11.7 0.7 %collective-permute-start.3 = (bf16[2,256,128]{2,1,0:T(8,128)(2,1)S(1)}, bf16[2,256,128]{2,1,0:T(8,128)(2,1)S(1)}, u32[]{:S(2)}, u32[]{:S(2)}) collective-permute-start(bf16[2,256,128]{2,1,0:T(8,128)(2,1)S(1)} %block.3.refs_1_), channel_id=1, source_target_pairs={{16,8},{17,9},{18,10},{19,11},{20,12},{21,13},{22,14},{23,15}} | collective-permute-start | bytes 393224 | tf_op jit(solution)/shard_map/ppermute | solution.py:345
  12.4 0.0 copy-done
  12.4 1.0 %collective-permute-start.7 = (bf16[2,1,64,256]{3,2,1,0:T(8,128)(2,1)S(1)}, bf16[2,1,64,256]{3,2,1,0:T(8,128)(2,1)S(1)}, u32[]{:S(2)}, u32[]{:S(2)}) collective-permute-start(bf16[2,1,64,256]{3,2,1,0:T(8,128)(2,1)S(1)} %bitcast.21), channel_id=1, source_target_pairs={{1,0},{0,1},{3,2},{2,3},{5,4},{4,5},{7,6},{6,7},{9,8},{8,9},{11,10... | collective-permute-start | bytes 196616 | tf_op jit(solution)/shard_map/ppermute | solution.py:27
  13.4 3.3 %collective-permute-done.7.refs_2_ = bf16[2,1,64,256]{3,2,1,0:T(8,128)(2,1)S(1)} collective-permute-done((bf16[2,1,64,256]{3,2,1,0:T(8,128)(2,1)S(1)}, bf16[2,1,64,256]{3,2,1,0:T(8,128)(2,1)S(1)}, u32[]{:S(2)}, u32[]{:S(2)}) %collective-permute-start.7) | collective-permute-done | bytes 65568 | tf_op jit(solution)/shard_map/ppermute | solution.py:27
  16.7 0.1 pack.1
  16.8 1.6 %collective-permute-start.8 = (bf16[2,320,128]{2,1,0:T(8,128)(2,1)S(1)}, bf16[2,320,128]{2,1,0:T(8,128)(2,1)S(1)}, u32[]{:S(2)}, u32[]{:S(2)}) collective-permute-start(bf16[2,320,128]{2,1,0:T(8,128)(2,1)S(1)} %get-tuple-element.29), channel_id=1, source_target_pairs={{4,0},{6,2},{0,4},{2,6},{5,1},{7,3},{1,5},{3,7},{12,8},{14,10},{8,... | collective-permute-start | bytes 491528 | tf_op jit(solution)/shard_map/ppermute | solution.py:357
  18.4 0.0 collective-permute-done.3.grad_ref.refs_2_
  18.4 1.4 %block.4.refs_2_ = bf16[2,256,128]{2,1,0:T(8,128)(2,1)S(1)} custom-call(bf16[2,256,128]{2,1,0:T(8,128)(2,1)S(1)} %collective-permute-done.3.grad_ref.refs_2_, bf16[2,256,128]{2,1,0:T(8,128)(2,1)S(1)} %get-tuple-element.26.pre_ref.refs_0_, bf16[27,256,256]{2,1,0:T(8,128)(2,1)S(1)} %get-tuple-element.23.refs_4_.conv_ref, ...), custom_call_target="tpu_custom_call" | custom-call | tf_op jit(solution)/shard_map/block/pallas_call | solution.py:364
  19.8 1.3 %collective-permute-start.4 = (bf16[2,256,128]{2,1,0:T(8,128)(2,1)S(1)}, bf16[2,256,128]{2,1,0:T(8,128)(2,1)S(1)}, u32[]{:S(2)}, u32[]{:S(2)}) collective-permute-start(bf16[2,256,128]{2,1,0:T(8,128)(2,1)S(1)} %block.4.refs_2_), channel_id=1, source_target_pairs={{8,0},{9,1},{10,2},{11,3},{12,4},{13,5},{14,6},{15,7}} | collective-permute-start | bytes 393224 | tf_op jit(solution)/shard_map/ppermute | solution.py:345
  21.1 0.1 collective-permute-start.9
  21.1 0.6 %collective-permute-start.10 = (bf16[2,320,128]{2,1,0:T(8,128)(2,1)S(1)}, bf16[2,320,128]{2,1,0:T(8,128)(2,1)S(1)}, u32[]{:S(2)}, u32[]{:S(2)}) collective-permute-start(bf16[2,320,128]{2,1,0:T(8,128)(2,1)S(1)} %get-tuple-element.32), channel_id=1, source_target_pairs={{2,0},{0,2},{6,4},{4,6},{3,1},{1,3},{7,5},{5,7},{10,8},{8,10},{14,... | collective-permute-start | bytes 491528 | tf_op jit(solution)/shard_map/ppermute | solution.py:357
  21.8 9.0 %collective-permute-done.4.grad_ref.refs_3_ = bf16[2,256,128]{2,1,0:T(8,128)(2,1)S(1)} collective-permute-done((bf16[2,256,128]{2,1,0:T(8,128)(2,1)S(1)}, bf16[2,256,128]{2,1,0:T(8,128)(2,1)S(1)}, u32[]{:S(2)}, u32[]{:S(2)}) %collective-permute-start.4) | collective-permute-done | bytes 131104 | tf_op jit(solution)/shard_map/ppermute | solution.py:345
  30.8 0.1 collective-permute-start.11
  30.9 1.6 %collective-permute-start.6 = (bf16[2,256,128]{2,1,0:T(8,128)(2,1)S(1)}, bf16[2,256,128]{2,1,0:T(8,128)(2,1)S(1)}, u32[]{:S(2)}, u32[]{:S(2)}) collective-permute-start(bf16[2,256,128]{2,1,0:T(8,128)(2,1)S(1)} %choose.1.refs_0_), channel_id=1, source_target_pairs={{6,0},{4,2},{2,4},{0,6},{7,1},{5,3},{3,5},{1,7},{14,8},{12,10},{10... | collective-permute-start | bytes 393224 | tf_op jit(solution)/shard_map/ppermute | solution.py:27
  32.5 0.0 collective-permute-done.8.refs_2_
  32.5 0.5 %collective-permute-start.5 = (bf16[2,256,128]{2,1,0:T(8,128)(2,1)S(1)}, bf16[2,256,128]{2,1,0:T(8,128)(2,1)S(1)}, u32[]{:S(2)}, u32[]{:S(2)}) collective-permute-start(bf16[2,256,128]{2,1,0:T(8,128)(2,1)S(1)} %choose.1.refs_0_), channel_id=1, source_target_pairs={{4,0},{6,2},{0,4},{2,6},{5,1},{7,3},{1,5},{3,7},{12,8},{14,10},{8,... | collective-permute-start | bytes 393224 | tf_op jit(solution)/shard_map/ppermute | solution.py:27
  33.1 0.0 collective-permute-done.9.refs_3_
  33.1 0.0 collective-permute-done.10.refs_1_.refs_3_
  33.1 0.4 unfold.1
  33.4 1.4 %block.5.refs_3_ = bf16[2,256,128]{2,1,0:T(8,128)(2,1)S(1)} custom-call(bf16[2,256,128]{2,1,0:T(8,128)(2,1)S(1)} %collective-permute-done.4.grad_ref.refs_3_, bf16[2,256,128]{2,1,0:T(8,128)(2,1)S(1)} %get-tuple-element.26.pre_ref.refs_0_, bf16[27,256,256]{2,1,0:T(8,128)(2,1)S(1)} %get-tuple-element.23.refs_4_.conv_ref, ...), custom_call_target="tpu_custom_call" | custom-call | tf_op jit(solution)/shard_map/block/pallas_call | solution.py:364
  34.8 0.8 %own_grads.1 = bf16[2,1,64,256]{3,2,1,0:T(8,128)(2,1)} custom-call(bf16[2,256,128]{2,1,0:T(8,128)(2,1)S(1)} %get-tuple-element.25.refs_0_, bf16[2,256,128]{2,1,0:T(8,128)(2,1)S(1)} %block.3.refs_1_, bf16[2,256,128]{2,1,0:T(8,128)(2,1)S(1)} %block.4.refs_2_, bf16[2,256,128]{2,1,0:T(8,128)(2,1)S(1)} %block.5.refs_3_), custom_call_target="tpu_custom_call" | custom-call | tf_op jit(solution)/shard_map/own_grads/pallas_call | solution.py:417
  35.6 0.0 collective-permute-done.11.refs_1_
  35.6 0.9 %near_weight_grads.1 = (f32[1728,256]{1,0:T(8,128)S(1)}, f32[64,256]{1,0:T(8,128)S(1)}) custom-call(bf16[2,256,128]{2,1,0:T(8,128)(2,1)S(1)} %choose.1.refs_0_, bf16[2,256,128]{2,1,0:T(8,128)(2,1)S(1)} %collective-permute-done.11.refs_1_, bf16[2,320,128]{2,1,0:T(8,128)(2,1)S(1)} %get-tuple-element.31.refs_0_.refs_2_, ...), custom_call_target="tpu_custom_call" | custom-call | tf_op jit(solution)/shard_map/near_weight_grads/pallas_call | solution.py:391
  36.5 0.0 collective-permute-done.6.refs_1_
  36.5 3.1 %collective-permute-done.5.refs_0_ = bf16[2,256,128]{2,1,0:T(8,128)(2,1)S(1)} collective-permute-done((bf16[2,256,128]{2,1,0:T(8,128)(2,1)S(1)}, bf16[2,256,128]{2,1,0:T(8,128)(2,1)S(1)}, u32[]{:S(2)}, u32[]{:S(2)}) %collective-permute-start.5) | collective-permute-done | bytes 131104 | tf_op jit(solution)/shard_map/ppermute | solution.py:27
  39.6 2.5 %far_weight_grads.1 = (f32[1728,256]{1,0:T(8,128)}, f32[64,256]{1,0:T(8,128)}) custom-call(bf16[2,256,128]{2,1,0:T(8,128)(2,1)S(1)} %collective-permute-done.5.refs_0_, bf16[2,256,128]{2,1,0:T(8,128)(2,1)S(1)} %collective-permute-done.6.refs_1_, bf16[2,320,128]{2,1,0:T(8,128)(2,1)S(1)} %collective-permute-done.8.refs_2_, ...), custom_call_target="tpu_custom_call" | custom-call | tf_op jit(solution)/shard_map/far_weight_grads/pallas_call | solution.py:403
  (1 shorter events, 0.0 us)
Async XLA Ops:
  0.6 5.6 %collective-permute-start.1 = (bf16[2,1,64,256]{3,2,1,0:T(8,128)(2,1)}, bf16[2,1,64,256]{3,2,1,0:T(8,128)(2,1)S(1)}, u32[]{:S(2)}, u32[]{:S(2)}) collective-permute-start(bf16[2,1,64,256]{3,2,1,0:T(8,128)(2,1)} %bitcast.16), channel_id=1, source_target_pairs={{1,0},{0,1},{3,2},{2,3},{5,4},{4,5},{7,6},{6,7},{9,8},{8,9},{11,10... | collective-permute-start | bytes 196616 | tf_op jit(solution)/shard_map/ppermute | solution.py:27
  3.7 4.5 %collective-permute-start = (bf16[2,1,64,256]{3,2,1,0:T(8,128)(2,1)}, bf16[2,1,64,256]{3,2,1,0:T(8,128)(2,1)S(1)}, u32[]{:S(2)}, u32[]{:S(2)}) collective-permute-start(bf16[2,1,64,256]{3,2,1,0:T(8,128)(2,1)} %bitcast.18), channel_id=1, source_target_pairs={{1,0},{0,1},{3,2},{2,3},{5,4},{4,5},{7,6},{6,7},{9,8},{8,9},{11,10... | collective-permute-start | bytes 196616 | tf_op jit(solution)/shard_map/ppermute | solution.py:27
  9.6 0.7 %collective-permute-start.2 = (bf16[2,256,128]{2,1,0:T(8,128)(2,1)S(1)}, bf16[2,256,128]{2,1,0:T(8,128)(2,1)S(1)}, u32[]{:S(2)}, u32[]{:S(2)}) collective-permute-start(bf16[2,256,128]{2,1,0:T(8,128)(2,1)S(1)} %get-tuple-element.25.refs_0_), channel_id=1, source_target_pairs={{24,16},{25,17},{26,18},{27,19},{28,20},{29,21},{30,22},{31,23}} | collective-permute-start | bytes 393224 | tf_op jit(solution)/shard_map/ppermute | solution.py:345
  10.3 2.1 %copy-start = (bf16[1,2,1,1,8,8,256]{6,5,4,3,2,1,0:T(8,128)(2,1)S(1)}, bf16[1,2,1,1,8,8,256]{6,5,4,3,2,1,0:T(8,128)(2,1)}, u32[]{:S(2)}) copy-start(bf16[1,2,1,1,8,8,256]{6,5,4,3,2,1,0:T(8,128)(2,1)} %param.5) | copy-start | bytes 196612
  11.7 6.7 %collective-permute-start.3 = (bf16[2,256,128]{2,1,0:T(8,128)(2,1)S(1)}, bf16[2,256,128]{2,1,0:T(8,128)(2,1)S(1)}, u32[]{:S(2)}, u32[]{:S(2)}) collective-permute-start(bf16[2,256,128]{2,1,0:T(8,128)(2,1)S(1)} %block.3.refs_1_), channel_id=1, source_target_pairs={{16,8},{17,9},{18,10},{19,11},{20,12},{21,13},{22,14},{23,15}} | collective-permute-start | bytes 393224 | tf_op jit(solution)/shard_map/ppermute | solution.py:345
  12.4 4.3 %collective-permute-start.7 = (bf16[2,1,64,256]{3,2,1,0:T(8,128)(2,1)S(1)}, bf16[2,1,64,256]{3,2,1,0:T(8,128)(2,1)S(1)}, u32[]{:S(2)}, u32[]{:S(2)}) collective-permute-start(bf16[2,1,64,256]{3,2,1,0:T(8,128)(2,1)S(1)} %bitcast.21), channel_id=1, source_target_pairs={{1,0},{0,1},{3,2},{2,3},{5,4},{4,5},{7,6},{6,7},{9,8},{8,9},{11,10... | collective-permute-start | bytes 196616 | tf_op jit(solution)/shard_map/ppermute | solution.py:27
  16.8 15.7 %collective-permute-start.8 = (bf16[2,320,128]{2,1,0:T(8,128)(2,1)S(1)}, bf16[2,320,128]{2,1,0:T(8,128)(2,1)S(1)}, u32[]{:S(2)}, u32[]{:S(2)}) collective-permute-start(bf16[2,320,128]{2,1,0:T(8,128)(2,1)S(1)} %get-tuple-element.29), channel_id=1, source_target_pairs={{4,0},{6,2},{0,4},{2,6},{5,1},{7,3},{1,5},{3,7},{12,8},{14,10},{8,... | collective-permute-start | bytes 491528 | tf_op jit(solution)/shard_map/ppermute | solution.py:357
  19.8 11.1 %collective-permute-start.4 = (bf16[2,256,128]{2,1,0:T(8,128)(2,1)S(1)}, bf16[2,256,128]{2,1,0:T(8,128)(2,1)S(1)}, u32[]{:S(2)}, u32[]{:S(2)}) collective-permute-start(bf16[2,256,128]{2,1,0:T(8,128)(2,1)S(1)} %block.4.refs_2_), channel_id=1, source_target_pairs={{8,0},{9,1},{10,2},{11,3},{12,4},{13,5},{14,6},{15,7}} | collective-permute-start | bytes 393224 | tf_op jit(solution)/shard_map/ppermute | solution.py:345
  21.1 12.0 %collective-permute-start.9 = (bf16[2,320,128]{2,1,0:T(8,128)(2,1)S(1)}, bf16[2,320,128]{2,1,0:T(8,128)(2,1)S(1)}, u32[]{:S(2)}, u32[]{:S(2)}) collective-permute-start(bf16[2,320,128]{2,1,0:T(8,128)(2,1)S(1)} %get-tuple-element.30), channel_id=1, source_target_pairs={{6,0},{4,2},{2,4},{0,6},{7,1},{5,3},{3,5},{1,7},{14,8},{12,10},{10... | collective-permute-start | bytes 491528 | tf_op jit(solution)/shard_map/ppermute | solution.py:357
  21.1 11.9 %collective-permute-start.10 = (bf16[2,320,128]{2,1,0:T(8,128)(2,1)S(1)}, bf16[2,320,128]{2,1,0:T(8,128)(2,1)S(1)}, u32[]{:S(2)}, u32[]{:S(2)}) collective-permute-start(bf16[2,320,128]{2,1,0:T(8,128)(2,1)S(1)} %get-tuple-element.32), channel_id=1, source_target_pairs={{2,0},{0,2},{6,4},{4,6},{3,1},{1,3},{7,5},{5,7},{10,8},{8,10},{14,... | collective-permute-start | bytes 491528 | tf_op jit(solution)/shard_map/ppermute | solution.py:357
  30.8 4.8 %collective-permute-start.11 = (bf16[2,256,128]{2,1,0:T(8,128)(2,1)S(1)}, bf16[2,256,128]{2,1,0:T(8,128)(2,1)S(1)}, u32[]{:S(2)}, u32[]{:S(2)}) collective-permute-start(bf16[2,256,128]{2,1,0:T(8,128)(2,1)S(1)} %choose.1.refs_0_), channel_id=1, source_target_pairs={{2,0},{0,2},{6,4},{4,6},{3,1},{1,3},{7,5},{5,7},{10,8},{8,10},{14,... | collective-permute-start | bytes 393224 | tf_op jit(solution)/shard_map/ppermute | solution.py:27
  30.9 5.5 %collective-permute-start.6 = (bf16[2,256,128]{2,1,0:T(8,128)(2,1)S(1)}, bf16[2,256,128]{2,1,0:T(8,128)(2,1)S(1)}, u32[]{:S(2)}, u32[]{:S(2)}) collective-permute-start(bf16[2,256,128]{2,1,0:T(8,128)(2,1)S(1)} %choose.1.refs_0_), channel_id=1, source_target_pairs={{6,0},{4,2},{2,4},{0,6},{7,1},{5,3},{3,5},{1,7},{14,8},{12,10},{10... | collective-permute-start | bytes 393224 | tf_op jit(solution)/shard_map/ppermute | solution.py:27
  32.5 7.1 %collective-permute-start.5 = (bf16[2,256,128]{2,1,0:T(8,128)(2,1)S(1)}, bf16[2,256,128]{2,1,0:T(8,128)(2,1)S(1)}, u32[]{:S(2)}, u32[]{:S(2)}) collective-permute-start(bf16[2,256,128]{2,1,0:T(8,128)(2,1)S(1)} %choose.1.refs_0_), channel_id=1, source_target_pairs={{4,0},{6,2},{0,4},{2,6},{5,1},{7,3},{1,5},{3,7},{12,8},{14,10},{8,... | collective-permute-start | bytes 393224 | tf_op jit(solution)/shard_map/ppermute | solution.py:27
